TPU v7x, 512 devices: a whole 4x4x16 slice. The times are simulated.
512 devices in a mesh: blk: 64 (over x, y, z_hi, core), row: 8 (over z_lo).
Axes of the slice: x: 4, y: 4, z: 16 (z_hi: 2, z_lo: 8; z = z_hi * 8 + z_lo), core: 2. Of those that a mesh axis runs over, the one named last changes fastest.
Arguments:
- amplitudes: bfloat16 [1152, 4, 1152], P('blk', None, 'row'), may hold values from -6 to 6
- cholesky: bfloat16 [64, 1152, 1152], P('blk'), may hold values from -0.109375 to 0.109375
- virt_irreps: int32 [1152], replicated, may hold values from 0 to 7, as said below
- pair_irreps: int32 [4], replicated, may hold values from 0 to 7
Outputs:
- ladder_sigma: bfloat16 [1152, 4, 1152], P('blk', None, 'row')
Inputs may be any that keep to these rules, and one draw needn't show every extreme that they name: `virt_irreps`: irreps of two orbitals combine by exclusive or; in each aligned block of 144 virtual orbitals no irrep holds more than 36 orbitals, and one irrep holds exactly 36. `pair_irreps`: one irrep per pair of the slab.
All inputs are finite; a program needn't handle non-finite values.
Results may differ from a plain program's by a relative error of at most 0.0049.
Values may be sent and summed in bfloat16 or wider, within the bound.
A program may use at most 64 MiB of HBM per device.

v0:
```python
import jax
import jax.numpy as jnp
from jax import lax
from jax.sharding import PartitionSpec as P


def allowed(irrep_rows, irrep_cols, pair_irreps):
    product = jnp.bitwise_xor(irrep_rows[:, None, None], irrep_cols[None, None, :])
    return product == pair_irreps[None, :, None]


def per_device(amplitudes, cholesky, virt_irreps, pair_irreps):
    vectors = cholesky[0]
    virt_count = vectors.shape[0]
    pair_count = amplitudes.shape[1]
    own_rows = amplitudes.shape[2]
    tile_rows = amplitudes.shape[0]
    row_first = lax.axis_index("row") * own_rows
    row_block = lax.dynamic_slice_in_dim(vectors, row_first, own_rows, 0)
    own_irreps = lax.dynamic_slice_in_dim(virt_irreps, row_first, own_rows, 0)
    widened = lax.all_gather(amplitudes, "row", axis=2, tiled=True)
    column_tile = lax.all_gather(widened, "blk", axis=0, tiled=True)
    allowed_in = allowed(virt_irreps, virt_irreps, pair_irreps)
    masked = jnp.where(allowed_in, column_tile, jnp.zeros_like(column_tile))
    contracted = jnp.einsum(
        "dpc,ac->dpa", masked, row_block, preferred_element_type=jnp.float32
    ).astype(jnp.bfloat16)
    flat_inner = contracted.reshape(virt_count, -1)
    col_first = lax.axis_index("blk") * tile_rows
    out_irreps = lax.dynamic_slice_in_dim(virt_irreps, col_first, tile_rows, 0)
    allowed_out = allowed(out_irreps, own_irreps, pair_irreps)
    summed = lax.psum_scatter(
        jnp.dot(vectors, flat_inner, preferred_element_type=jnp.float32),
        "blk",
        scatter_dimension=0,
        tiled=True,
    )
    summed = summed.reshape(tile_rows, pair_count, own_rows)
    return jnp.where(allowed_out, summed, jnp.zeros_like(summed)).astype(jnp.bfloat16)


def solution(mesh):
    placed = (P("blk", None, "row"), P("blk", None, None), P(), P())
    return jax.shard_map(
        per_device, mesh=mesh, in_specs=placed, out_specs=P("blk", None, "row"), check_vma=False
    )
```

profile of v0, /device:TPU:1, one launch (start us, length us, event | category | flops | bytes accessed | tf_op | source)
XLA Modules:
  0.0 950.6 jit_solution(16580209991946468367)
XLA Ops:
  6.5 0.0 copy-start
  6.5 0.0 copy-start.1
  6.5 0.0 all-gather.2.cloned.1.call-start
  6.5 1.1 copy.7
  7.7 52.3 %all_gather.6 = bf16[18,4,1152]{0,1,2:T(4,128)(2,1)} all-gather(bf16[18,4,144]{0,1,2:T(4,128)(2,1)S(1)} %copy.7), channel_id=1, replica_groups=mesh['blk'=64,'row'=8] {'row'}, dimensions={2}, use_global_device_ids=true | all-gather | bytes 186624 | tf_op jit(solution)/shard_map/all_gather | solution.py:21
  60.0 2.7 copy.8
  62.7 0.0 all-gather.2.cloned.1.call-update
  62.7 0.8 dynamic_slice.12
  63.5 0.8 dynamic_slice.11
  64.2 1.3 dynamic-slice.1
  66.2 0.1 broadcast_xor_fusion.1
  66.2 3.6 broadcast_xor_fusion
  69.8 193.9 %all-gather.2.cloned.1.call-done = bf16[1152,4,1152]{2,1,0:T(4,128)(2,1)} async-done(((bf16[18,4,1152]{2,1,0:T(4,128)(2,1)}), bf16[1152,4,1152]{2,1,0:T(4,128)(2,1)}) %all-gather.2.cloned.1.call-update) | async-done | bytes 10616848 | tf_op jit(solution)/shard_map/all_gather | solution.py:22
  263.7 0.0 copy-done.1
  263.7 12.8 %compare_select_fusion = bf16[1152,4,1152]{2,1,0:T(4,128)(2,1)S(1)} fusion(bf16[1152,4,1152]{2,1,0:T(4,128)(2,1)} %all-gather.2.cloned.1.call-done, s32[1152,1152]{1,0:T(8,128)} %broadcast_xor_fusion, s32[4]{0:T(128)S(1)} %copy-done.1), kind=kLoop, calls=%fused_computation | loop fusion | flops 10616832 | bytes 26542096 | tf_op jit(solution)/shard_map/jit(_where)/select_n | solution.py:24
  276.5 0.0 copy-done
  276.5 3.3 fusion.2
  279.8 3.6 convolution_bitcast_fusion
  283.4 658.4 %all-reduce.2 = bf16[1152,576]{0,1:T(8,128)(2,1)} all-reduce(f32[1152,576]{0,1:T(8,128)} %convolution_bitcast_fusion), channel_id=2, replica_groups=mesh['blk'=64,'row'=8] {'blk'}, use_global_device_ids=true, to_apply=%region_0.1.clone | all-reduce | flops 663552 | bytes 3981312
  941.8 1.1 constant_dynamic-slice_fusion
  942.8 0.1 copy.10
  943.0 0.7 select_convert_fusion
Async XLA Ops:
  6.5 270.0 %copy-start = (bf16[1,1152,1152]{2,1,0:T(8,128)(2,1)S(1)}, bf16[1,1152,1152]{2,1,0:T(8,128)(2,1)}, u32[]{:S(2)}) copy-start(bf16[1,1152,1152]{2,1,0:T(8,128)(2,1)} %param.5) | copy-start | bytes 7962628
  6.5 257.1 %copy-start.1 = (s32[4]{0:T(128)S(1)}, s32[4]{0:T(128)}, u32[]{:S(2)}) copy-start(s32[4]{0:T(128)} %param.7) | copy-start | bytes 52
  6.5 257.1 %all-gather.2.cloned.1.call-start = ((), (), s32[]{:S(2)}) async-start(), calls=%async_computation | async-start | bytes 10782720 | tf_op jit(solution)/shard_map/all_gather | solution.py:22
Sparse Core Ops, SparseCore 0:
  62.8 200.8 all-gather.1
where the time goes:
time: 966 us; the launch traced here: 951 us
  blocking collectives  711 us (74%)
  waiting for transfers between devices  194 us (20%)
  other arithmetic  17.2 us (2%)
  between operations  14.1 us (1%)
    unnamed x1, blocking collectives  658 us
    all_gather x1, waiting for transfers between devices, per_device(): column_tile = lax.all_gather(widened, 'blk', axis=0, tiled=True)  194 us
    all_gather x1, blocking collectives, per_device(): widened = lax.all_gather(amplitudes, 'row', axis=2, tiled=True)  52.3 us
  transfers between devices with their start and end apart: 1, of which 1 were waited for; matrix products, arithmetic and copies ran while one was open for 1% of the time, Pallas kernels for 0%

commit v1 on v0

v1 whole, which is shorter than its diff:
```python
import jax
import jax.numpy as jnp
from jax import lax
from jax.experimental import pallas as pl
from jax.experimental.pallas import tpu as pltpu
from jax.sharding import PartitionSpec as P

NV = 1152
BLK = 144
TILE = 18
HALF = 576
CHIP = 72
ROW4 = 288
F32 = jnp.float32
BF16 = jnp.bfloat16
I32 = jnp.int32
MESH = pl.DeviceIdType.MESH


def iota(shape, dim):
    return lax.broadcasted_iota(I32, shape, dim)


def dot(a, b):
    return jnp.dot(a, b, preferred_element_type=F32)


def dot_nt(a, b):
    return lax.dot_general(a, b, (((1,), (1,)), ((), ())), preferred_element_type=F32)


def lane_key(lane):
    main = ((lane >> 5) << 6) + (lane & 31)
    tail = (((lane >> 2) & 3) << 6) + 32 + (lane & 3)
    return jnp.where(lane < 128, main, tail)


def over36(v):
    return (v >= 36).astype(I32) + (v >= 72).astype(I32) + (v >= 108).astype(I32)


def kernel(
    amp_ref, chol_ref, irr_ref, pair_ref, out_ref,
    vec, irrblk, rankblk, irrhalf, rankrow, rankhalf, colg, x32, own, rpack,
    lanek, expand, reduce_r, tailsel, tx1, rx1, gathered, texp, inner, outgoing,
    sibling, summed, rx3, tx4, rx4,
    vec_sem, s1_send, s1_recv, s2_send, s2_fwd, s2_recv, s3_sib_send, s3_sib_recv,
    s3_send, s3_recv, s4_send, s4_recv,
):
    j = lax.axis_index("blk")
    r = lax.axis_index("row")
    m, zh, core = j // 4, (j // 2) % 2, j % 2
    x, y = m // 4, m % 4
    p, h = r // 2, r % 2
    other = 4 * m + 2 * zh + (1 - core)

    load_vec = pltpu.make_async_copy(chol_ref.at[0], vec, vec_sem)
    load_vec.start()

    barrier = pltpu.get_barrier_semaphore()

    def greet_line(t, c):
        @pl.when(jnp.logical_or(t // 8 != 2 * zh + core, t % 8 != r))
        def _():
            pl.semaphore_signal(barrier, inc=1, device_id=(4 * m + t // 8, t % 8), device_id_type=MESH)
        return c

    lax.fori_loop(0, 32, greet_line, 0)

    def peer(o):
        return 4 * ((x + o // 4) % 4) + (y + o) % 4

    def source(o):
        return 4 * ((x + 4 - o // 4) % 4) + (y + 4 - o % 4) % 4

    def greet_plane(o, c):
        pl.semaphore_signal(barrier, inc=1, device_id=(4 * peer(o) + 2 * zh + core, r), device_id_type=MESH)
        return c

    lax.fori_loop(1, 16, greet_plane, 0)

    irr = irr_ref[...]
    upper = (iota((BLK, BLK), 0) < iota((BLK, BLK), 1)).astype(BF16)
    eye = iota((BLK, BLK), 0) == iota((BLK, BLK), 1)
    ones = jnp.ones((BLK, 128), BF16)
    pair_own = pair_ref[p]
    members = []
    for b in range(8):
        irr_b = irr[:, BLK * b : BLK * (b + 1)]
        irrblk[b : b + 1, :] = irr_b
        members.append((jnp.broadcast_to(irr_b, (8, BLK)) == iota((8, BLK), 0)).astype(F32))
        diagonal = jnp.where(eye, jnp.broadcast_to(irr_b, (BLK, BLK)), 0).astype(F32).astype(BF16)
        column = dot(diagonal, ones).astype(I32)
        colg[BLK * b : BLK * (b + 1), :] = jnp.bitwise_xor(column, pair_own)
    irrhalf[0:1, :] = irr[:, :HALF]
    irrhalf[1:2, :] = irr[:, HALF:]
    members = jnp.concatenate(members, axis=0)
    before = members * dot(members.astype(BF16), upper)
    for b in range(8):
        rank_b = jnp.sum(before[8 * b : 8 * b + 8], axis=0, keepdims=True).astype(I32)
        rankblk[b : b + 1, :] = rank_b
        keyed = rank_b + 64 * b
        rankrow[:, BLK * b : BLK * (b + 1)] = keyed
    rankhalf[0:1, :] = rankrow[:, :HALF]
    rankhalf[1:2, :] = rankrow[:, HALF:] - 256

    row72 = iota((CHIP, 1), 0)
    own_index = TILE * j + (row72 >> 2)
    own_irr = jnp.sum(
        jnp.where(iota((CHIP, NV), 1) == own_index, jnp.broadcast_to(irr, (CHIP, NV)), 0).astype(F32),
        axis=1, keepdims=True,
    ).astype(I32)
    pairs_col = jnp.zeros((CHIP, 1), I32)
    for q in range(4):
        pairs_col = jnp.where((row72 & 3) == q, pair_ref[q], pairs_col)
    own_goal = jnp.bitwise_xor(own_irr, pairs_col)
    own_mask = (own_goal == irrblk[pl.ds(r, 1), :]).astype(F32)
    own[...] = own_mask
    lane128 = iota((128, BLK), 0)
    slot128 = lane128 - 36 * over36(lane128)
    rpack[...] = jnp.logical_and(lane128 < 108, slot128 == rankblk[pl.ds(r, 1), :]).astype(BF16)
    for dd in range(TILE):
        x32[4 * dd : 4 * dd + 4, :] = amp_ref[dd].astype(F32)
    masked = (x32[...] * own_mask).astype(BF16)
    lane_group = over36(iota((CHIP, 128), 1))
    third = iota((CHIP, 128), 0)
    third = (third >= 24).astype(I32) + (third >= 48).astype(I32)
    spread = jnp.where(lane_group == third, dot_nt(masked, rpack[...]), 0.0).astype(BF16)
    pk_row, pk_col = iota((32, CHIP), 0), iota((32, CHIP), 1)
    col_third = (pk_col >= 24).astype(I32) + (pk_col >= 48).astype(I32)
    pick = jnp.logical_and(
        (pk_row >> 3) == (pk_col & 3), (pk_row & 7) == (pk_col >> 2) - 6 * col_third
    ).astype(BF16)
    packed = dot(pick, spread)
    for q in range(4):
        tx1[q] = packed[8 * q : 8 * q + 8]

    pl.semaphore_wait(barrier, 46)

    slot_me = (r % 4) * 4 + 2 * zh + core

    def s1_copy(t):
        return pltpu.make_async_remote_copy(
            src_ref=tx1.at[(t % 8) // 2], dst_ref=rx1.at[slot_me],
            send_sem=s1_send.at[t], recv_sem=s1_recv,
            device_id=(4 * m + 2 * (t // 8) + r // 4, t % 8), device_id_type=MESH,
        )

    def s1_is_me(t):
        return jnp.logical_and(core == r // 4, jnp.logical_and(t // 8 == zh, t % 8 == r))

    def s1_start(t, c):
        me = s1_is_me(t)

        @pl.when(jnp.logical_not(me))
        def _():
            s1_copy(t).start()

        @pl.when(me)
        def _():
            pltpu.make_async_copy(tx1.at[p], rx1.at[slot_me], s1_recv).start()
        return c

    lax.fori_loop(0, 16, s1_start, 0)

    col = iota((1, 768), 1)
    key = lane_key(col & 255)
    target = (key >> 6) * 128 + 36 * (col >> 8) + (key & 63)
    lanek[...] = (iota((512, 768), 0) == target).astype(BF16)
    lane_col = iota((512, 1), 0)
    expand[...] = (lane_key(lane_col & 255) + 256 * (lane_col >> 8) == rankrow[...]).astype(BF16)
    reduce_r[...] = (lane_key(iota((256, 1), 0)) == rankhalf[pl.ds(h, 1), :]).astype(BF16)
    ts_row, ts_col = iota((320, 64), 0), iota((320, 64), 1)
    tailsel[...] = jnp.logical_and(
        (ts_row >> 3) == 10 * (ts_col >> 4) + (ts_col & 15), (ts_col & 15) < 10
    ).astype(BF16)
    u_row, u_lane = iota((ROW4, 128), 0), iota((ROW4, 128), 1)
    u_match = (u_row & 7) == (u_lane >> 4)
    u_match320 = (iota((320, 128), 0) & 7) == (iota((320, 128), 1) >> 4)

    def row_target(c):
        return TILE * ((c >> 3) & 3) + 6 * (c >> 5) + (c & 7)

    rs_row, rs_col = iota((80, 96), 0), iota((80, 96), 1)
    rowsel = jnp.logical_and(rs_row == row_target(rs_col), (rs_col & 7) < 6).astype(BF16)
    rt_row, rt_col = iota((96, 80), 0), iota((96, 80), 1)
    rowsel_t = jnp.logical_and(rt_col == row_target(rt_row), (rt_row & 7) < 6).astype(BF16)
    tail_pack = ((iota((16, 80), 1) >> 3) == iota((16, 80), 0)).astype(BF16)
    tp_row, tp_col = iota((64, ROW4), 0), iota((64, ROW4), 1)
    tail_pack4 = jnp.logical_and(
        (tp_col >> 3) == 9 * (tp_row >> 4) + (tp_row & 15), (tp_row & 15) < 9
    ).astype(BF16)

    pltpu.make_async_copy(rx1, rx1, s1_recv).wait()
    arrived = jnp.concatenate([rx1[s] for s in range(16)], axis=0)
    wide = jnp.concatenate([arrived[32 * g : 32 * g + 32] for g in range(4)], axis=1).astype(BF16)
    placed = dot(wide, lanek[...]).astype(BF16)
    stacked = jnp.concatenate([placed[:, 256 * k : 256 * k + 256] for k in range(3)], axis=0)
    rows = dot(rowsel, stacked)
    gathered[core, m, 0:80] = rows[:, :128].astype(BF16)
    tails = jnp.where(u_match320[:80], rows[:, 128:], 0.0).astype(BF16)
    gathered[core, m, 80:96] = dot(tail_pack, tails).astype(BF16)

    def s2_copy(o):
        return pltpu.make_async_remote_copy(
            src_ref=gathered.at[core, m], dst_ref=gathered.at[core, m],
            send_sem=s2_send.at[o], recv_sem=s2_recv.at[core, m],
            device_id=(4 * peer(o) + 2 * zh + core, r), device_id_type=MESH,
        )

    def s2_pass(o):
        src = source(o)
        return pltpu.make_async_remote_copy(
            src_ref=gathered.at[core, src], dst_ref=gathered.at[core, src],
            send_sem=s2_fwd.at[o], recv_sem=s2_recv.at[core, src],
            device_id=(other, r), device_id_type=MESH,
        )

    def arrival(part, src):
        return pltpu.make_async_copy(gathered.at[part, src], gathered.at[part, src], s2_recv.at[part, src])

    def s2_start(o, c):
        s2_copy(o).start()
        return c

    lax.fori_loop(1, 16, s2_start, 0)
    s2_pass(0).start()

    def hand_on(o, c):
        arrival(core, source(o)).wait()
        s2_pass(o).start()
        return c

    lax.fori_loop(1, 4, hand_on, 0)
    load_vec.wait()

    def chunk_in(q, c):
        @pl.when(q < 3)
        def _():
            lax.fori_loop(4 * q + 4, 4 * q + 8, hand_on, 0)

        xs = (x + 4 - q) % 4

        def wait_sibling(o, c2):
            arrival(1 - core, source(o)).wait()
            return c2

        lax.fori_loop(4 * q, 4 * q + 4, wait_sibling, 0)
        parts = []
        for half in range(2):
            main = jnp.concatenate([gathered[half, 4 * xs + k, 0:80] for k in range(4)], axis=0)
            tail = jnp.concatenate([gathered[half, 4 * xs + k, 80:96] for k in range(4)], axis=0)
            tail = jnp.where(u_match320, dot(tailsel[...], tail), 0.0).astype(BF16)
            parts.append(jnp.concatenate([main, tail], axis=1))
        first = pl.multiple_of(ROW4 * xs, ROW4)
        goal = colg[pl.ds(first, ROW4), :]

        def put(begin, end, value):
            value = jnp.concatenate([value[80 * k : 80 * k + CHIP] for k in range(4)], axis=0)
            width = end - begin
            wide_goal = jnp.concatenate([goal] * (width // 128), axis=1)
            keep = wide_goal == irr_ref[:, begin:end]
            texp[:, begin:end] = jnp.where(keep, value, 0.0).astype(BF16)

        put(0, 512, dot(parts[0], expand[0:256, 0:512]))
        put(512, 768, dot(jnp.concatenate(parts, axis=1), expand[:, 512:768]))
        put(768, 1152, dot(parts[1], expand[256:512, 768:1152]))
        rows_h = vec[pl.ds(pl.multiple_of(HALF * h, HALF), HALF), :]
        inner[pl.ds(first, ROW4), :] = dot_nt(texp[...], rows_h).astype(BF16)
        return c

    lax.fori_loop(0, 4, chunk_in, 0)

    def sib_copy(d):
        return pltpu.make_async_remote_copy(
            src_ref=outgoing.at[d], dst_ref=sibling.at[d // 2],
            send_sem=s3_sib_send.at[d // 2], recv_sem=s3_sib_recv.at[d // 2],
            device_id=(other, r), device_id_type=MESH,
        )

    def s3_copy(d):
        return pltpu.make_async_remote_copy(
            src_ref=summed.at[d // 2], dst_ref=rx3.at[m],
            send_sem=s3_send.at[d // 2], recv_sem=s3_recv.at[m],
            device_id=(4 * d + 2 * zh + core, r), device_id_type=MESH,
        )

    def merge(q):
        xd = (x + q + 1) % 4
        for e in range(2):
            d = 4 * xd + 2 * e + core
            slot = 2 * xd + e
            pltpu.make_async_copy(sibling.at[slot], sibling.at[slot], s3_sib_recv.at[slot]).wait()
            total = (outgoing[d].astype(F32) + sibling[slot].astype(F32)).astype(BF16)

            @pl.when(d == m)
            def _():
                rx3[m] = total

            @pl.when(d != m)
            def _():
                summed[slot] = total
                s3_copy(d).start()

    def chunk_out(q, c):
        xd = (x + q + 1) % 4
        first = pl.multiple_of(ROW4 * xd, ROW4)
        sig = dot(vec[pl.ds(first, ROW4), :], inner[...])
        goal = colg[pl.ds(first, ROW4), :]
        wide_goal = jnp.concatenate([goal] * 4 + [goal[:, :64]], axis=1)
        keep = wide_goal == irrhalf[pl.ds(h, 1), :]
        sig = jnp.where(keep, sig, 0.0).astype(BF16)
        short = dot_nt(sig, reduce_r[...])
        tail = jnp.where(u_match, short[:, 128:], 0.0).astype(BF16)
        tail = dot(tail_pack4, tail)
        for k in range(4):
            block = jnp.concatenate([short[CHIP * k : CHIP * k + CHIP, :128], jnp.zeros((8, 128), F32)], axis=0)
            outgoing[4 * xd + k, 0:80] = block.astype(BF16)
            outgoing[4 * xd + k, 80:96] = tail[16 * k : 16 * k + 16].astype(BF16)
        for e in range(2):
            sib_copy(4 * xd + 2 * e + 1 - core).start()

        @pl.when(q > 0)
        def _():
            merge(q - 1)
        return c

    lax.fori_loop(0, 4, chunk_out, 0)
    merge(3)

    def s4_copy(t):
        return pltpu.make_async_remote_copy(
            src_ref=tx4.at[t], dst_ref=rx4.at[2 * p + zh],
            send_sem=s4_send.at[t], recv_sem=s4_recv,
            device_id=(4 * m + t % 4, 4 * h + t // 4), device_id_type=MESH,
        )

    def s4_is_me(t):
        return jnp.logical_and(t % 4 == 2 * zh + core, 4 * h + t // 4 == r)

    reducer = core == y % 2

    @pl.when(reducer)
    def _():
        def take(o, c):
            src = source(o)
            pltpu.make_async_copy(rx3.at[src], rx3.at[src], s3_recv.at[src]).wait()
            return c

        lax.fori_loop(1, 16, take, 0)
        total = rx3[0].astype(F32)
        for s in range(1, 16):
            total = total + rx3[s].astype(F32)
        high = total.astype(BF16)
        low = (total - high.astype(F32)).astype(BF16)
        result = jnp.zeros((32, 512), F32)
        for piece in (high, low):
            tail = jnp.where(u_match320[:80], dot(tailsel[0:80, 0:16], piece[80:96]), 0.0).astype(BF16)
            full = jnp.concatenate([piece[0:80], tail], axis=1)
            by_row = dot(rowsel_t, full).astype(BF16)
            by_row = jnp.concatenate([by_row[32 * k : 32 * k + 32] for k in range(3)], axis=1)
            result = result + dot_nt(by_row, lanek[...])
        for t in range(16):
            tx4[t] = result[8 * (t % 4) : 8 * (t % 4) + 8, 128 * (t // 4) : 128 * (t // 4) + 128]

        def s4_start(t, c):
            me = s4_is_me(t)

            @pl.when(jnp.logical_not(me))
            def _():
                s4_copy(t).start()

            @pl.when(me)
            def _():
                pltpu.make_async_copy(tx4.at[t], rx4.at[2 * p + zh], s4_recv).start()
            return c

        lax.fori_loop(0, 16, s4_start, 0)

    pltpu.make_async_copy(rx4, rx4, s4_recv).wait()
    got = jnp.concatenate([rx4[2 * q] + rx4[2 * q + 1] for q in range(4)], axis=0).astype(BF16)
    up_row, up_col = iota((CHIP, 32), 0), iota((CHIP, 32), 1)
    up_third = (up_row >= 24).astype(I32) + (up_row >= 48).astype(I32)
    unpick = jnp.logical_and(
        (up_col >> 3) == (up_row & 3), (up_col & 7) == (up_row >> 2) - 6 * up_third
    ).astype(BF16)
    spread_out = jnp.where(lane_group == third, dot(unpick, got), 0.0).astype(BF16)
    final = dot(spread_out, rpack[...]) * own[...]
    for dd in range(TILE):
        out_ref[dd] = final[4 * dd : 4 * dd + 4, :].astype(BF16)

    def s1_done(t, c):
        @pl.when(jnp.logical_not(s1_is_me(t)))
        def _():
            s1_copy(t).wait_send()
        return c

    lax.fori_loop(0, 16, s1_done, 0)
    s2_pass(0).wait_send()

    def s2_done(o, c):
        s2_copy(o).wait_send()
        s2_pass(o).wait_send()
        return c

    lax.fori_loop(1, 16, s2_done, 0)

    def s3_done(n, c):
        sib_copy(2 * n + 1 - core).wait_send()

        @pl.when(2 * n + core != m)
        def _():
            s3_copy(2 * n + core).wait_send()
        return c

    lax.fori_loop(0, 8, s3_done, 0)

    @pl.when(reducer)
    def _():
        def s4_done(t, c):
            @pl.when(jnp.logical_not(s4_is_me(t)))
            def _():
                s4_copy(t).wait_send()
            return c

        lax.fori_loop(0, 16, s4_done, 0)


def per_device(amplitudes, cholesky, virt_irreps, pair_irreps):
    vmem = pl.BlockSpec(memory_space=pltpu.VMEM)
    dma, reg = pltpu.SemaphoreType.DMA, pltpu.SemaphoreType.REGULAR
    return pl.pallas_call(
        kernel,
        out_shape=jax.ShapeDtypeStruct(amplitudes.shape, BF16),
        in_specs=[vmem, pl.BlockSpec(memory_space=pl.ANY), vmem, pl.BlockSpec(memory_space=pltpu.SMEM)],
        out_specs=vmem,
        scratch_shapes=[
            pltpu.VMEM((NV, NV), BF16),
            pltpu.VMEM((8, BLK), I32),
            pltpu.VMEM((8, BLK), I32),
            pltpu.VMEM((8, HALF), I32),
            pltpu.VMEM((1, NV), I32),
            pltpu.VMEM((8, HALF), I32),
            pltpu.VMEM((NV, 128), I32),
            pltpu.VMEM((CHIP, BLK), F32),
            pltpu.VMEM((CHIP, BLK), F32),
            pltpu.VMEM((128, BLK), BF16),
            pltpu.VMEM((512, 768), BF16),
            pltpu.VMEM((512, NV), BF16),
            pltpu.VMEM((256, HALF), BF16),
            pltpu.VMEM((320, 64), BF16),
            pltpu.VMEM((4, 8, 128), F32),
            pltpu.VMEM((16, 8, 128), F32),
            pltpu.VMEM((2, 16, 96, 128), BF16),
            pltpu.VMEM((ROW4, NV), BF16),
            pltpu.VMEM((NV, HALF), BF16),
            pltpu.VMEM((16, 96, 128), BF16),
            pltpu.VMEM((8, 96, 128), BF16),
            pltpu.VMEM((8, 96, 128), BF16),
            pltpu.VMEM((16, 96, 128), BF16),
            pltpu.VMEM((16, 8, 128), F32),
            pltpu.VMEM((8, 8, 128), F32),
            dma,
            dma((16,)), dma,
            dma((16,)), dma((16,)), dma((2, 16)),
            dma((8,)), dma((8,)),
            dma((8,)), dma((16,)),
            dma((16,)), dma,
        ],
        compiler_params=pltpu.CompilerParams(
            collective_id=0, has_side_effects=True, vmem_limit_bytes=40 * 1024 * 1024
        ),
        cost_estimate=pl.CostEstimate(flops=3_060_000_000, bytes_accessed=2_700_000, transcendentals=0),
    )(amplitudes, cholesky, virt_irreps.reshape(1, NV), pair_irreps)


def solution(mesh):
    placed = (P("blk", None, "row"), P("blk", None, None), P(), P())
    return jax.shard_map(
        per_device, mesh=mesh, in_specs=placed, out_specs=P("blk", None, "row"), check_vma=False
    )
```

time: 966 us -> 61.2 us (0.06); the launches traced: 951 us -> 60.9 us
  blocking collectives: 711 us -> 0 us
  waiting for transfers between devices: 194 us -> 0 us
  Pallas kernels: 0 us -> 56.4 us
  other arithmetic: 17.2 us -> 0 us
  between operations: 14.1 us -> 0.01 us
    unnamed x1 -> x0, blocking collectives: 658 us -> none
    all_gather x1 -> x0, waiting for transfers between devices: 194 us -> none  [per_device(): column_tile = lax.all_gather(widened, 'blk', axis=0, tiled=True)]
    pallas_call x0 -> x1, Pallas kernels: none -> 56.4 us  [per_device(): pl.pallas_call(kernel, out_shape=jax.ShapeDtypeStruct(amplitudes.shape, B...]
    all_gather x1 -> x0, blocking collectives: 52.3 us -> none  [per_device(): widened = lax.all_gather(amplitudes, 'row', axis=2, tiled=True)]
    select_n x1 -> x0, other arithmetic: 12.8 us -> none  [per_device(): masked = jnp.where(allowed_in, column_tile, jnp.zeros_like(column_tile))]
  transfers between devices with their start and end apart: 1 -> 0, of which waited for: 1 -> 0; matrix products, arithmetic and copies ran while one was open for 1% -> 0% of each run, Pallas kernels for 0% -> 0%
where the time goes in v1:
time: 61.2 us; the launch traced here: 60.9 us
  Pallas kernels  56.4 us (92%)
  local copies, waits for them, and re-layouts  4.49 us (7%)
    pallas_call x1, Pallas kernels, per_device(): pl.pallas_call(kernel, out_shape=jax.ShapeDtypeStruct(amplitudes.shape, B...  56.4 us
    unnamed x7, local copies, waits for them, and re-layouts  3.79 us

profile of v1, /device:TPU:1, one launch (start us, length us, event | category | flops | bytes accessed | tf_op | source)
XLA Modules:
  0.0 60.9 jit_solution(5670710774929653100)
XLA Ops:
  0.0 0.7 %reshape.3.irr_ref = s32[1,1152]{1,0:T(1,128)S(1)} reshape(s32[1152]{0:T(1024)} %param.6) | data formatting | bytes 9216 | tf_op jit(solution)/shard_map/reshape | solution.py:474
  0.7 0.0 copy-start
  0.7 1.7 %copy-done = bf16[1,1152,1152]{2,1,0:T(8,128)(2,1)S(1)} copy-done((bf16[1,1152,1152]{2,1,0:T(8,128)(2,1)S(1)}, bf16[1,1152,1152]{2,1,0:T(8,128)(2,1)}, u32[]{:S(2)}) %copy-start) | copy-done | bytes 2654232
  2.5 0.0 copy-start.1
  2.5 0.8 %copy-done.1 = bf16[18,4,144]{2,1,0:T(4,128)(2,1)S(1)} copy-done((bf16[18,4,144]{2,1,0:T(4,128)(2,1)S(1)}, bf16[18,4,144]{2,1,0:T(4,128)(2,1)}, u32[]{:S(2)}) %copy-start.1) | copy-done | bytes 20760
  3.2 0.0 copy-start.2
  3.2 0.7 %copy-done.2 = s32[4]{0:T(128)S(1)} copy-done((s32[4]{0:T(128)S(1)}, s32[4]{0:T(128)}, u32[]{:S(2)}) %copy-start.2) | copy-done | bytes 40
  3.9 56.4 %shard_map.46 = bf16[18,4,144]{2,1,0:T(4,128)(2,1)S(1)} custom-call(bf16[18,4,144]{2,1,0:T(4,128)(2,1)S(1)} %copy-done.1, bf16[1,1152,1152]{2,1,0:T(8,128)(2,1)S(1)} %copy-done, s32[1,1152]{1,0:T(1,128)S(1)} %reshape.3.irr_ref, s32[4]{0:T(128)S(1)} %copy-done.2), custom_call_target="tpu_custom_call" | custom-call | flops 3060000000 | bytes 2700000 | tf_op jit(solution)/shard_map/pallas_call | solution.py:432
  60.3 0.6 %copy.6 = bf16[18,4,144]{2,1,0:T(4,128)(2,1)} copy(bf16[18,4,144]{2,1,0:T(4,128)(2,1)S(1)} %shard_map.46) | data formatting | bytes 41472
Async XLA Ops:
  0.7 1.7 %copy-start = (bf16[1,1152,1152]{2,1,0:T(8,128)(2,1)S(1)}, bf16[1,1152,1152]{2,1,0:T(8,128)(2,1)}, u32[]{:S(2)}) copy-start(bf16[1,1152,1152]{2,1,0:T(8,128)(2,1)} %chol_ref.1) | copy-start | bytes 7962628
  2.5 0.8 %copy-start.1 = (bf16[18,4,144]{2,1,0:T(4,128)(2,1)S(1)}, bf16[18,4,144]{2,1,0:T(4,128)(2,1)}, u32[]{:S(2)}) copy-start(bf16[18,4,144]{2,1,0:T(4,128)(2,1)} %amp_ref.1) | copy-start | bytes 62212
  3.2 0.7 %copy-start.2 = (s32[4]{0:T(128)S(1)}, s32[4]{0:T(128)}, u32[]{:S(2)}) copy-start(s32[4]{0:T(128)} %pair_ref.1) | copy-start | bytes 52

commit v2 on v1

--- a/solution.py
+++ b/solution.py
@@ -40,46 +40,67 @@
 
 
 def kernel(
-    amp_ref, chol_ref, irr_ref, pair_ref, out_ref,
-    vec, irrblk, rankblk, irrhalf, rankrow, rankhalf, colg, x32, own, rpack,
+    amp_hbm, chol_ref, irr_hbm, pair_hbm, out_ref,
+    amp_ref, irr9, pair_ref, irr_ref, vec, irrblk, rankblk, irrhalf, rankrow, rankhalf, colg, x32, own, rpack,
     lanek, expand, reduce_r, tailsel, tx1, rx1, gathered, texp, inner, outgoing,
     sibling, summed, rx3, tx4, rx4,
-    vec_sem, s1_send, s1_recv, s2_send, s2_fwd, s2_recv, s3_sib_send, s3_sib_recv,
+    vec_sem, small_sem, s1_send, s1_recv, s2_send, s2_fwd, s2_recv, s3_sib_send, s3_sib_recv,
     s3_send, s3_recv, s4_send, s4_recv,
 ):
     j = lax.axis_index("blk")
     r = lax.axis_index("row")
     m, zh, core = j // 4, (j // 2) % 2, j % 2
     x, y = m // 4, m % 4
-    p, h = r // 2, r % 2
+    p, h = r % 4, 1 - r // 4
+    z = 8 * zh + r
     other = 4 * m + 2 * zh + (1 - core)
 
     load_vec = pltpu.make_async_copy(chol_ref.at[0], vec, vec_sem)
+    loads = [
+        pltpu.make_async_copy(irr_hbm, irr9, small_sem.at[0]),
+        pltpu.make_async_copy(pair_hbm, pair_ref, small_sem.at[1]),
+        pltpu.make_async_copy(amp_hbm, amp_ref, small_sem.at[2]),
+    ]
+    for load in loads:
+        load.start()
     load_vec.start()
 
     barrier = pltpu.get_barrier_semaphore()
 
+    def ring_far(t):
+        return 8 + (t // 2) * (1 - 2 * (t % 2)) - t % 2
+
     def greet_line(t, c):
-        @pl.when(jnp.logical_or(t // 8 != 2 * zh + core, t % 8 != r))
-        def _():
-            pl.semaphore_signal(barrier, inc=1, device_id=(4 * m + t // 8, t % 8), device_id_type=MESH)
-        return c
-
-    lax.fori_loop(0, 32, greet_line, 0)
+        zd = (z + ring_far(t)) % 16
+        for k in range(2):
+            @pl.when(jnp.logical_or(t < 15, core != k))
+            def _():
+                pl.semaphore_signal(
+                    barrier, inc=1, device_id=(4 * m + 2 * (zd // 8) + k, zd % 8), device_id_type=MESH
+                )
+        return c
+
+    lax.fori_loop(0, 16, greet_line, 0)
+
+    def far(i):
+        return 2 + i // 2 - (i % 2) * (1 + 2 * (i // 2))
 
     def peer(o):
-        return 4 * ((x + o // 4) % 4) + (y + o) % 4
+        return 4 * ((x + far(o // 4)) % 4) + (y + far(o % 4)) % 4
 
     def source(o):
-        return 4 * ((x + 4 - o // 4) % 4) + (y + 4 - o % 4) % 4
+        return 4 * ((x + 4 - far(o // 4)) % 4) + (y + 4 - far(o % 4)) % 4
 
     def greet_plane(o, c):
         pl.semaphore_signal(barrier, inc=1, device_id=(4 * peer(o) + 2 * zh + core, r), device_id_type=MESH)
         return c
 
-    lax.fori_loop(1, 16, greet_plane, 0)
-
-    irr = irr_ref[...]
+    lax.fori_loop(0, 15, greet_plane, 0)
+
+    for load in loads:
+        load.wait()
+    irr = jnp.concatenate([irr9[k : k + 1, :] for k in range(9)], axis=1)
+    irr_ref[...] = irr
     upper = (iota((BLK, BLK), 0) < iota((BLK, BLK), 1)).astype(BF16)
     eye = iota((BLK, BLK), 0) == iota((BLK, BLK), 1)
     ones = jnp.ones((BLK, 128), BF16)
@@ -140,14 +161,15 @@
     slot_me = (r % 4) * 4 + 2 * zh + core
 
     def s1_copy(t):
-        return pltpu.make_async_remote_copy(
-            src_ref=tx1.at[(t % 8) // 2], dst_ref=rx1.at[slot_me],
+        zd = (z + ring_far(t)) % 16
+        return pltpu.make_async_remote_copy(
+            src_ref=tx1.at[zd % 4], dst_ref=rx1.at[slot_me],
             send_sem=s1_send.at[t], recv_sem=s1_recv,
-            device_id=(4 * m + 2 * (t // 8) + r // 4, t % 8), device_id_type=MESH,
+            device_id=(4 * m + 2 * (zd // 8) + r // 4, zd % 8), device_id_type=MESH,
         )
 
     def s1_is_me(t):
-        return jnp.logical_and(core == r // 4, jnp.logical_and(t // 8 == zh, t % 8 == r))
+        return jnp.logical_and(core == r // 4, t == 15)
 
     def s1_start(t, c):
         me = s1_is_me(t)
@@ -223,23 +245,23 @@
         s2_copy(o).start()
         return c
 
-    lax.fori_loop(1, 16, s2_start, 0)
-    s2_pass(0).start()
+    lax.fori_loop(0, 15, s2_start, 0)
+    s2_pass(15).start()
 
     def hand_on(o, c):
         arrival(core, source(o)).wait()
         s2_pass(o).start()
         return c
 
-    lax.fori_loop(1, 4, hand_on, 0)
+    lax.fori_loop(0, 4, hand_on, 0)
     load_vec.wait()
 
     def chunk_in(q, c):
         @pl.when(q < 3)
         def _():
-            lax.fori_loop(4 * q + 4, 4 * q + 8, hand_on, 0)
-
-        xs = (x + 4 - q) % 4
+            lax.fori_loop(4 * q + 4, 4 * q + 8 - q // 2, hand_on, 0)
+
+        xs = (x + 4 - far(q)) % 4
 
         def wait_sibling(o, c2):
             arrival(1 - core, source(o)).wait()
@@ -286,7 +308,7 @@
         )
 
     def merge(q):
-        xd = (x + q + 1) % 4
+        xd = (x + far(q)) % 4
         for e in range(2):
             d = 4 * xd + 2 * e + core
             slot = 2 * xd + e
@@ -303,7 +325,7 @@
                 s3_copy(d).start()
 
     def chunk_out(q, c):
-        xd = (x + q + 1) % 4
+        xd = (x + far(q)) % 4
         first = pl.multiple_of(ROW4 * xd, ROW4)
         sig = dot(vec[pl.ds(first, ROW4), :], inner[...])
         goal = colg[pl.ds(first, ROW4), :]
@@ -329,14 +351,12 @@
     merge(3)
 
     def s4_copy(t):
+        rr, tile = t // 4, t % 4
         return pltpu.make_async_remote_copy(
             src_ref=tx4.at[t], dst_ref=rx4.at[2 * p + zh],
             send_sem=s4_send.at[t], recv_sem=s4_recv,
-            device_id=(4 * m + t % 4, 4 * h + t // 4), device_id_type=MESH,
-        )
-
-    def s4_is_me(t):
-        return jnp.logical_and(t % 4 == 2 * zh + core, 4 * h + t // 4 == r)
+            device_id=(4 * m + tile, 4 * h + rr), device_id_type=MESH,
+        )
 
     reducer = core == y % 2
 
@@ -347,35 +367,62 @@
             pltpu.make_async_copy(rx3.at[src], rx3.at[src], s3_recv.at[src]).wait()
             return c
 
-        lax.fori_loop(1, 16, take, 0)
+        lax.fori_loop(0, 15, take, 0)
         total = rx3[0].astype(F32)
         for s in range(1, 16):
             total = total + rx3[s].astype(F32)
-        high = total.astype(BF16)
-        low = (total - high.astype(F32)).astype(BF16)
-        result = jnp.zeros((32, 512), F32)
-        for piece in (high, low):
-            tail = jnp.where(u_match320[:80], dot(tailsel[0:80, 0:16], piece[80:96]), 0.0).astype(BF16)
-            full = jnp.concatenate([piece[0:80], tail], axis=1)
-            by_row = dot(rowsel_t, full).astype(BF16)
-            by_row = jnp.concatenate([by_row[32 * k : 32 * k + 32] for k in range(3)], axis=1)
-            result = result + dot_nt(by_row, lanek[...])
+        total = total.astype(BF16)
+        tail = jnp.where(u_match320[:80], dot(tailsel[0:80, 0:16], total[80:96]), 0.0).astype(BF16)
+        by_row = dot(rowsel_t, jnp.concatenate([total[0:80], tail], axis=1)).astype(BF16)
+        by_row = jnp.concatenate([by_row[32 * k : 32 * k + 32] for k in range(3)], axis=1)
+        result = dot_nt(by_row, lanek[...])
         for t in range(16):
             tx4[t] = result[8 * (t % 4) : 8 * (t % 4) + 8, 128 * (t // 4) : 128 * (t // 4) + 128]
 
         def s4_start(t, c):
-            me = s4_is_me(t)
-
-            @pl.when(jnp.logical_not(me))
+            zd = (z + ring_far(t)) % 16
+
+            @pl.when((zd % 8) // 4 == h)
             def _():
-                s4_copy(t).start()
-
-            @pl.when(me)
-            def _():
-                pltpu.make_async_copy(tx4.at[t], rx4.at[2 * p + zh], s4_recv).start()
+                for k in range(2):
+                    s4_copy(4 * (zd % 4) + 2 * (zd // 8) + k).start()
             return c
 
         lax.fori_loop(0, 16, s4_start, 0)
+
+    def s1_done(t, c):
+        @pl.when(jnp.logical_not(s1_is_me(t)))
+        def _():
+            s1_copy(t).wait_send()
+        return c
+
+    lax.fori_loop(0, 16, s1_done, 0)
+    s2_pass(15).wait_send()
+
+    def s2_done(o, c):
+        s2_copy(o).wait_send()
+        s2_pass(o).wait_send()
+        return c
+
+    lax.fori_loop(0, 15, s2_done, 0)
+
+    def s3_done(n, c):
+        sib_copy(2 * n + 1 - core).wait_send()
+
+        @pl.when(2 * n + core != m)
+        def _():
+            s3_copy(2 * n + core).wait_send()
+        return c
+
+    lax.fori_loop(0, 8, s3_done, 0)
+
+    @pl.when(reducer)
+    def _():
+        def s4_done(t, c):
+            s4_copy(t).wait_send()
+            return c
+
+        lax.fori_loop(0, 16, s4_done, 0)
 
     pltpu.make_async_copy(rx4, rx4, s4_recv).wait()
     got = jnp.concatenate([rx4[2 * q] + rx4[2 * q + 1] for q in range(4)], axis=0).astype(BF16)
@@ -389,52 +436,20 @@
     for dd in range(TILE):
         out_ref[dd] = final[4 * dd : 4 * dd + 4, :].astype(BF16)
 
-    def s1_done(t, c):
-        @pl.when(jnp.logical_not(s1_is_me(t)))
-        def _():
-            s1_copy(t).wait_send()
-        return c
-
-    lax.fori_loop(0, 16, s1_done, 0)
-    s2_pass(0).wait_send()
-
-    def s2_done(o, c):
-        s2_copy(o).wait_send()
-        s2_pass(o).wait_send()
-        return c
-
-    lax.fori_loop(1, 16, s2_done, 0)
-
-    def s3_done(n, c):
-        sib_copy(2 * n + 1 - core).wait_send()
-
-        @pl.when(2 * n + core != m)
-        def _():
-            s3_copy(2 * n + core).wait_send()
-        return c
-
-    lax.fori_loop(0, 8, s3_done, 0)
-
-    @pl.when(reducer)
-    def _():
-        def s4_done(t, c):
-            @pl.when(jnp.logical_not(s4_is_me(t)))
-            def _():
-                s4_copy(t).wait_send()
-            return c
-
-        lax.fori_loop(0, 16, s4_done, 0)
-
 
 def per_device(amplitudes, cholesky, virt_irreps, pair_irreps):
     vmem = pl.BlockSpec(memory_space=pltpu.VMEM)
-    dma, reg = pltpu.SemaphoreType.DMA, pltpu.SemaphoreType.REGULAR
+    dma = pltpu.SemaphoreType.DMA
     return pl.pallas_call(
         kernel,
         out_shape=jax.ShapeDtypeStruct(amplitudes.shape, BF16),
-        in_specs=[vmem, pl.BlockSpec(memory_space=pl.ANY), vmem, pl.BlockSpec(memory_space=pltpu.SMEM)],
+        in_specs=[pl.BlockSpec(memory_space=pltpu.HBM)] * 4,
         out_specs=vmem,
         scratch_shapes=[
+            pltpu.VMEM((TILE, 4, BLK), BF16),
+            pltpu.VMEM((9, 128), I32),
+            pltpu.SMEM((4,), I32),
+            pltpu.VMEM((1, NV), I32),
             pltpu.VMEM((NV, NV), BF16),
             pltpu.VMEM((8, BLK), I32),
             pltpu.VMEM((8, BLK), I32),
@@ -460,7 +475,7 @@
             pltpu.VMEM((16, 96, 128), BF16),
             pltpu.VMEM((16, 8, 128), F32),
             pltpu.VMEM((8, 8, 128), F32),
-            dma,
+            dma, dma((3,)),
             dma((16,)), dma,
             dma((16,)), dma((16,)), dma((2, 16)),
             dma((8,)), dma((8,)),
@@ -468,10 +483,10 @@
             dma((16,)), dma,
         ],
         compiler_params=pltpu.CompilerParams(
-            collective_id=0, has_side_effects=True, vmem_limit_bytes=40 * 1024 * 1024
+            collective_id=0, has_side_effects=True, vmem_limit_bytes=62 * 1024 * 1024
         ),
         cost_estimate=pl.CostEstimate(flops=3_060_000_000, bytes_accessed=2_700_000, transcendentals=0),
-    )(amplitudes, cholesky, virt_irreps.reshape(1, NV), pair_irreps)
+    )(amplitudes, cholesky, virt_irreps.reshape(9, 128), pair_irreps)
 
 
 def solution(mesh):

time: 61.2 us -> 56.6 us (0.925)
  local copies, waits for them, and re-layouts: 4.49 us -> 1.4 us
  Pallas kernels: 56.4 us -> 55.1 us
    unnamed x7 -> x1, local copies, waits for them, and re-layouts: 3.79 us -> 1.4 us
    pallas_call x1, Pallas kernels: 56.4 us -> 55.1 us  [per_device(): pl.pallas_call(kernel, out_shape=jax.ShapeDtypeStruct(amplitudes.shape, B...]
    reshape x1 -> x0, local copies, waits for them, and re-layouts: 0.7 us -> none  [per_device(): virt_irreps.reshape(1, NV)]
where the time goes in v2:
time: 56.6 us; the launch traced here: 56.5 us
  Pallas kernels  55.1 us (97%)
  local copies, waits for them, and re-layouts  1.4 us (2%)
    pallas_call x1, Pallas kernels, per_device(): pl.pallas_call(kernel, out_shape=jax.ShapeDtypeStruct(amplitudes.shape, B...  55.1 us
    unnamed x1, local copies, waits for them, and re-layouts  1.4 us

profile of v2, /device:TPU:1, one launch (start us, length us, event | category | flops | bytes accessed | tf_op | source)
XLA Modules:
  0.0 56.5 jit_solution(2010788953485474109)
XLA Ops:
  0.0 55.1 %shard_map.46 = bf16[18,4,144]{2,1,0:T(4,128)(2,1)} custom-call(bf16[18,4,144]{2,1,0:T(4,128)(2,1)} %amp_hbm.1, bf16[1,1152,1152]{2,1,0:T(8,128)(2,1)} %chol_ref.1, s32[9,128]{1,0:T(8,128)} %bitcast.1, s32[4]{0:T(128)} %pair_hbm.1), custom_call_target="tpu_custom_call" | custom-call | flops 3060000000 | bytes 2700000 | tf_op jit(solution)/shard_map/pallas_call | solution.py:443
  55.1 1.4 %copy.6 = bf16[18,4,144]{2,1,0:T(4,128)(2,1)} copy(bf16[18,4,144]{2,1,0:T(4,128)(2,1)} %shard_map.46) | data formatting | bytes 41472

commit v3 on v2

--- a/solution.py
+++ b/solution.py
@@ -86,10 +86,10 @@
         return 2 + i // 2 - (i % 2) * (1 + 2 * (i // 2))
 
     def peer(o):
-        return 4 * ((x + far(o // 4)) % 4) + (y + far(o % 4)) % 4
+        return 4 * ((x + far(o % 4)) % 4) + (y + far(o // 4)) % 4
 
     def source(o):
-        return 4 * ((x + 4 - far(o // 4)) % 4) + (y + 4 - far(o % 4)) % 4
+        return 4 * ((x + 4 - far(o % 4)) % 4) + (y + 4 - far(o // 4)) % 4
 
     def greet_plane(o, c):
         pl.semaphore_signal(barrier, inc=1, device_id=(4 * peer(o) + 2 * zh + core, r), device_id_type=MESH)
@@ -172,7 +172,10 @@
         return jnp.logical_and(core == r // 4, t == 15)
 
     def s1_start(t, c):
-        me = s1_is_me(t)
+        if t < 15:
+            s1_copy(t).start()
+            return c
+        me = core == r // 4
 
         @pl.when(jnp.logical_not(me))
         def _():
@@ -183,7 +186,8 @@
             pltpu.make_async_copy(tx1.at[p], rx1.at[slot_me], s1_recv).start()
         return c
 
-    lax.fori_loop(0, 16, s1_start, 0)
+    for t in range(16):
+        s1_start(t, 0)
 
     col = iota((1, 768), 1)
     key = lane_key(col & 255)
@@ -207,6 +211,9 @@
     rowsel = jnp.logical_and(rs_row == row_target(rs_col), (rs_col & 7) < 6).astype(BF16)
     rt_row, rt_col = iota((96, 80), 0), iota((96, 80), 1)
     rowsel_t = jnp.logical_and(rt_col == row_target(rt_row), (rt_row & 7) < 6).astype(BF16)
+    rq_row, rq_col = iota((96, 16), 0), iota((96, 16), 1)
+    rowsel_tail = jnp.logical_and(rq_col == row_target(rq_row) >> 3, (rq_row & 7) < 6).astype(BF16)
+    row_u = (row_target(iota((96, 128), 0)) & 7) == (iota((96, 128), 1) >> 4)
     tail_pack = ((iota((16, 80), 1) >> 3) == iota((16, 80), 0)).astype(BF16)
     tp_row, tp_col = iota((64, ROW4), 0), iota((64, ROW4), 1)
     tail_pack4 = jnp.logical_and(
@@ -245,7 +252,8 @@
         s2_copy(o).start()
         return c
 
-    lax.fori_loop(0, 15, s2_start, 0)
+    for o in range(15):
+        s2_start(o, 0)
     s2_pass(15).start()
 
     def hand_on(o, c):
@@ -253,45 +261,37 @@
         s2_pass(o).start()
         return c
 
-    lax.fori_loop(0, 4, hand_on, 0)
+    lax.fori_loop(0, 15, hand_on, 0)
     load_vec.wait()
 
-    def chunk_in(q, c):
-        @pl.when(q < 3)
-        def _():
-            lax.fori_loop(4 * q + 4, 4 * q + 8 - q // 2, hand_on, 0)
-
-        xs = (x + 4 - far(q)) % 4
-
-        def wait_sibling(o, c2):
-            arrival(1 - core, source(o)).wait()
-            return c2
-
-        lax.fori_loop(4 * q, 4 * q + 4, wait_sibling, 0)
-        parts = []
-        for half in range(2):
-            main = jnp.concatenate([gathered[half, 4 * xs + k, 0:80] for k in range(4)], axis=0)
-            tail = jnp.concatenate([gathered[half, 4 * xs + k, 80:96] for k in range(4)], axis=0)
-            tail = jnp.where(u_match320, dot(tailsel[...], tail), 0.0).astype(BF16)
-            parts.append(jnp.concatenate([main, tail], axis=1))
-        first = pl.multiple_of(ROW4 * xs, ROW4)
-        goal = colg[pl.ds(first, ROW4), :]
-
-        def put(begin, end, value):
-            value = jnp.concatenate([value[80 * k : 80 * k + CHIP] for k in range(4)], axis=0)
-            width = end - begin
-            wide_goal = jnp.concatenate([goal] * (width // 128), axis=1)
-            keep = wide_goal == irr_ref[:, begin:end]
-            texp[:, begin:end] = jnp.where(keep, value, 0.0).astype(BF16)
-
-        put(0, 512, dot(parts[0], expand[0:256, 0:512]))
-        put(512, 768, dot(jnp.concatenate(parts, axis=1), expand[:, 512:768]))
-        put(768, 1152, dot(parts[1], expand[256:512, 768:1152]))
-        rows_h = vec[pl.ds(pl.multiple_of(HALF * h, HALF), HALF), :]
-        inner[pl.ds(first, ROW4), :] = dot_nt(texp[...], rows_h).astype(BF16)
-        return c
-
-    lax.fori_loop(0, 4, chunk_in, 0)
+    def wait_sibling(o, c):
+        arrival(1 - core, source(o)).wait()
+        return c
+
+    lax.fori_loop(0, 16, wait_sibling, 0)
+
+    u_all = (iota((1280, 128), 0) & 7) == (iota((1280, 128), 1) >> 4)
+    parts = []
+    for half in range(2):
+        main = jnp.concatenate([gathered[half, chip, 0:80] for chip in range(16)], axis=0)
+        tail = jnp.concatenate([
+            dot(tailsel[...], jnp.concatenate([gathered[half, 4 * g + k, 80:96] for k in range(4)], axis=0))
+            for g in range(4)
+        ], axis=0)
+        tail = jnp.where(u_all, tail, 0.0).astype(BF16)
+        parts.append(jnp.concatenate([main, tail], axis=1))
+
+    def put(begin, end, value):
+        value = jnp.concatenate([value[80 * k : 80 * k + CHIP] for k in range(16)], axis=0)
+        wide_goal = jnp.concatenate([colg[...]] * ((end - begin) // 128), axis=1)
+        keep = wide_goal == irr_ref[:, begin:end]
+        texp[:, begin:end] = jnp.where(keep, value, 0.0).astype(BF16)
+
+    put(0, 512, dot(parts[0], expand[0:256, 0:512]))
+    put(512, 768, dot(jnp.concatenate(parts, axis=1), expand[:, 512:768]))
+    put(768, 1152, dot(parts[1], expand[256:512, 768:1152]))
+    rows_h = vec[pl.ds(pl.multiple_of(HALF * h, HALF), HALF), :]
+    inner[...] = dot_nt(texp[...], rows_h).astype(BF16)
 
     def sib_copy(d):
         return pltpu.make_async_remote_copy(
@@ -303,7 +303,7 @@
     def s3_copy(d):
         return pltpu.make_async_remote_copy(
             src_ref=summed.at[d // 2], dst_ref=rx3.at[m],
-            send_sem=s3_send.at[d // 2], recv_sem=s3_recv.at[m],
+            send_sem=s3_send.at[d // 2], recv_sem=s3_recv,
             device_id=(4 * d + 2 * zh + core, r), device_id_type=MESH,
         )
 
@@ -324,7 +324,7 @@
                 summed[slot] = total
                 s3_copy(d).start()
 
-    def chunk_out(q, c):
+    def chunk_out(q):
         xd = (x + far(q)) % 4
         first = pl.multiple_of(ROW4 * xd, ROW4)
         sig = dot(vec[pl.ds(first, ROW4), :], inner[...])
@@ -342,12 +342,11 @@
         for e in range(2):
             sib_copy(4 * xd + 2 * e + 1 - core).start()
 
-        @pl.when(q > 0)
-        def _():
+        if q:
             merge(q - 1)
-        return c
-
-    lax.fori_loop(0, 4, chunk_out, 0)
+
+    for q in range(4):
+        chunk_out(q)
     merge(3)
 
     def s4_copy(t):
@@ -362,18 +361,13 @@
 
     @pl.when(reducer)
     def _():
-        def take(o, c):
-            src = source(o)
-            pltpu.make_async_copy(rx3.at[src], rx3.at[src], s3_recv.at[src]).wait()
-            return c
-
-        lax.fori_loop(0, 15, take, 0)
+        pltpu.make_async_copy(rx3.at[0:15], rx3.at[0:15], s3_recv).wait()
         total = rx3[0].astype(F32)
         for s in range(1, 16):
             total = total + rx3[s].astype(F32)
         total = total.astype(BF16)
-        tail = jnp.where(u_match320[:80], dot(tailsel[0:80, 0:16], total[80:96]), 0.0).astype(BF16)
-        by_row = dot(rowsel_t, jnp.concatenate([total[0:80], tail], axis=1)).astype(BF16)
+        tail = jnp.where(row_u, dot(rowsel_tail, total[80:96]), 0.0).astype(BF16)
+        by_row = jnp.concatenate([dot(rowsel_t, total[0:80]).astype(BF16), tail], axis=1)
         by_row = jnp.concatenate([by_row[32 * k : 32 * k + 32] for k in range(3)], axis=1)
         result = dot_nt(by_row, lanek[...])
         for t in range(16):
@@ -388,7 +382,8 @@
                     s4_copy(4 * (zd % 4) + 2 * (zd // 8) + k).start()
             return c
 
-        lax.fori_loop(0, 16, s4_start, 0)
+        for t in range(16):
+            s4_start(t, 0)
 
     def s1_done(t, c):
         @pl.when(jnp.logical_not(s1_is_me(t)))
@@ -467,7 +462,7 @@
             pltpu.VMEM((4, 8, 128), F32),
             pltpu.VMEM((16, 8, 128), F32),
             pltpu.VMEM((2, 16, 96, 128), BF16),
-            pltpu.VMEM((ROW4, NV), BF16),
+            pltpu.VMEM((NV, NV), BF16),
             pltpu.VMEM((NV, HALF), BF16),
             pltpu.VMEM((16, 96, 128), BF16),
             pltpu.VMEM((8, 96, 128), BF16),
@@ -479,7 +474,7 @@
             dma((16,)), dma,
             dma((16,)), dma((16,)), dma((2, 16)),
             dma((8,)), dma((8,)),
-            dma((8,)), dma((16,)),
+            dma((8,)), dma,
             dma((16,)), dma,
         ],
         compiler_params=pltpu.CompilerParams(

time: 56.6 us -> 55.6 us (0.982)
  Pallas kernels: 55.1 us -> 54 us
    pallas_call x1, Pallas kernels: 55.1 us -> 54 us  [per_device(): pl.pallas_call(kernel, out_shape=jax.ShapeDtypeStruct(amplitudes.shape, B...]
where the time goes in v3:
time: 55.6 us; the launch traced here: 55.4 us
  Pallas kernels  54 us (97%)
  local copies, waits for them, and re-layouts  1.4 us (3%)
    pallas_call x1, Pallas kernels, per_device(): pl.pallas_call(kernel, out_shape=jax.ShapeDtypeStruct(amplitudes.shape, B...  54 us
    unnamed x1, local copies, waits for them, and re-layouts  1.4 us

profile of v3, /device:TPU:1, one launch (start us, length us, event | category | flops | bytes accessed | tf_op | source)
XLA Modules:
  0.0 55.4 jit_solution(673748896428367115)
XLA Ops:
  0.0 54.0 %shard_map.46 = bf16[18,4,144]{2,1,0:T(4,128)(2,1)} custom-call(bf16[18,4,144]{2,1,0:T(4,128)(2,1)} %amp_hbm.1, bf16[1,1152,1152]{2,1,0:T(8,128)(2,1)} %chol_ref.1, s32[9,128]{1,0:T(8,128)} %bitcast.1, s32[4]{0:T(128)} %pair_hbm.1), custom_call_target="tpu_custom_call" | custom-call | flops 3060000000 | bytes 2700000 | tf_op jit(solution)/shard_map/pallas_call | solution.py:438
  54.0 1.4 %copy.6 = bf16[18,4,144]{2,1,0:T(4,128)(2,1)} copy(bf16[18,4,144]{2,1,0:T(4,128)(2,1)} %shard_map.46) | data formatting | bytes 41472

commit v4 on v3

--- a/solution.py
+++ b/solution.py
@@ -293,25 +293,27 @@
     rows_h = vec[pl.ds(pl.multiple_of(HALF * h, HALF), HALF), :]
     inner[...] = dot_nt(texp[...], rows_h).astype(BF16)
 
+    def slot_of(d):
+        return (d // 8) * 4 + d % 4
+
     def sib_copy(d):
         return pltpu.make_async_remote_copy(
-            src_ref=outgoing.at[d], dst_ref=sibling.at[d // 2],
-            send_sem=s3_sib_send.at[d // 2], recv_sem=s3_sib_recv.at[d // 2],
+            src_ref=outgoing.at[d], dst_ref=sibling.at[slot_of(d)],
+            send_sem=s3_sib_send.at[slot_of(d)], recv_sem=s3_sib_recv.at[slot_of(d)],
             device_id=(other, r), device_id_type=MESH,
         )
 
     def s3_copy(d):
         return pltpu.make_async_remote_copy(
-            src_ref=summed.at[d // 2], dst_ref=rx3.at[m],
-            send_sem=s3_send.at[d // 2], recv_sem=s3_recv,
+            src_ref=summed.at[slot_of(d)], dst_ref=rx3.at[m],
+            send_sem=s3_send.at[slot_of(d)], recv_sem=s3_recv,
             device_id=(4 * d + 2 * zh + core, r), device_id_type=MESH,
         )
 
-    def merge(q):
-        xd = (x + far(q)) % 4
-        for e in range(2):
-            d = 4 * xd + 2 * e + core
-            slot = 2 * xd + e
+    def merge(xd):
+        for k in range(4):
+            d = 4 * xd + k
+            slot = slot_of(d)
             pltpu.make_async_copy(sibling.at[slot], sibling.at[slot], s3_sib_recv.at[slot]).wait()
             total = (outgoing[d].astype(F32) + sibling[slot].astype(F32)).astype(BF16)
 
@@ -324,8 +326,7 @@
                 summed[slot] = total
                 s3_copy(d).start()
 
-    def chunk_out(q):
-        xd = (x + far(q)) % 4
+    def chunk_out(xd):
         first = pl.multiple_of(ROW4 * xd, ROW4)
         sig = dot(vec[pl.ds(first, ROW4), :], inner[...])
         goal = colg[pl.ds(first, ROW4), :]
@@ -339,15 +340,17 @@
             block = jnp.concatenate([short[CHIP * k : CHIP * k + CHIP, :128], jnp.zeros((8, 128), F32)], axis=0)
             outgoing[4 * xd + k, 0:80] = block.astype(BF16)
             outgoing[4 * xd + k, 80:96] = tail[16 * k : 16 * k + 16].astype(BF16)
-        for e in range(2):
-            sib_copy(4 * xd + 2 * e + 1 - core).start()
-
-        if q:
-            merge(q - 1)
-
-    for q in range(4):
-        chunk_out(q)
-    merge(3)
+
+    even = (x + core) % 2
+    for k in range(2):
+        xd = (x + 2 - 2 * k + 1 - even) % 4
+        chunk_out(xd)
+        for n in range(4):
+            sib_copy(4 * xd + n).start()
+    for k in range(2):
+        xd = (x + 2 - 2 * k + even) % 4
+        chunk_out(xd)
+        merge(xd)
 
     def s4_copy(t):
         rr, tile = t // 4, t % 4
@@ -357,7 +360,7 @@
             device_id=(4 * m + tile, 4 * h + rr), device_id_type=MESH,
         )
 
-    reducer = core == y % 2
+    reducer = core == x % 2
 
     @pl.when(reducer)
     def _():
@@ -402,11 +405,12 @@
     lax.fori_loop(0, 15, s2_done, 0)
 
     def s3_done(n, c):
-        sib_copy(2 * n + 1 - core).wait_send()
-
-        @pl.when(2 * n + core != m)
+        sib_copy(8 * (n // 4) + 4 * (1 - core) + n % 4).wait_send()
+        d = 8 * (n // 4) + 4 * core + n % 4
+
+        @pl.when(d != m)
         def _():
-            s3_copy(2 * n + core).wait_send()
+            s3_copy(d).wait_send()
         return c
 
     lax.fori_loop(0, 8, s3_done, 0)

time: 55.6 us -> 55.1 us (level)
  no operation moved by 1% of the time
where the time goes in v4:
time: 55.1 us; the launch traced here: 54.9 us
  Pallas kernels  53.5 us (97%)
  local copies, waits for them, and re-layouts  1.4 us (3%)
    pallas_call x1, Pallas kernels, per_device(): pl.pallas_call(kernel, out_shape=jax.ShapeDtypeStruct(amplitudes.shape, B...  53.5 us
    unnamed x1, local copies, waits for them, and re-layouts  1.4 us

profile of v4, /device:TPU:1, one launch (start us, length us, event | category | flops | bytes accessed | tf_op | source)
XLA Modules:
  0.0 54.9 jit_solution(15053800288349992780)
XLA Ops:
  0.0 53.5 %shard_map.46 = bf16[18,4,144]{2,1,0:T(4,128)(2,1)} custom-call(bf16[18,4,144]{2,1,0:T(4,128)(2,1)} %amp_hbm.1, bf16[1,1152,1152]{2,1,0:T(8,128)(2,1)} %chol_ref.1, s32[9,128]{1,0:T(8,128)} %bitcast.1, s32[4]{0:T(128)} %pair_hbm.1), custom_call_target="tpu_custom_call" | custom-call | flops 3060000000 | bytes 2700000 | tf_op jit(solution)/shard_map/pallas_call | solution.py:442
  53.5 1.4 %copy.6 = bf16[18,4,144]{2,1,0:T(4,128)(2,1)} copy(bf16[18,4,144]{2,1,0:T(4,128)(2,1)} %shard_map.46) | data formatting | bytes 41472

commit v5 on v4

--- a/solution.py
+++ b/solution.py
@@ -42,7 +42,7 @@
 def kernel(
     amp_hbm, chol_ref, irr_hbm, pair_hbm, out_ref,
     amp_ref, irr9, pair_ref, irr_ref, vec, irrblk, rankblk, irrhalf, rankrow, rankhalf, colg, x32, own, rpack,
-    lanek, expand, reduce_r, tailsel, tx1, rx1, gathered, texp, inner, outgoing,
+    vec_t, irrpad, lanek, expand, reduce_r, tailsel, tx1, rx1, gathered, texp, inner, outgoing,
     sibling, summed, rx3, tx4, rx4,
     vec_sem, small_sem, s1_send, s1_recv, s2_send, s2_fwd, s2_recv, s3_sib_send, s3_sib_recv,
     s3_send, s3_recv, s4_send, s4_recv,
@@ -193,8 +193,11 @@
     key = lane_key(col & 255)
     target = (key >> 6) * 128 + 36 * (col >> 8) + (key & 63)
     lanek[...] = (iota((512, 768), 0) == target).astype(BF16)
-    lane_col = iota((512, 1), 0)
-    expand[...] = (lane_key(lane_col & 255) + 256 * (lane_col >> 8) == rankrow[...]).astype(BF16)
+    empty = jnp.full((1, 64), -1, I32)
+    for half in range(2):
+        irrpad[half : half + 1, :] = jnp.concatenate([irrhalf[half : half + 1, :], empty], axis=1)
+        keys = jnp.concatenate([rankhalf[half : half + 1, :], empty], axis=1)
+        expand[half] = (lane_key(iota((256, 1), 0)) == keys).astype(BF16)
     reduce_r[...] = (lane_key(iota((256, 1), 0)) == rankhalf[pl.ds(h, 1), :]).astype(BF16)
     ts_row, ts_col = iota((320, 64), 0), iota((320, 64), 1)
     tailsel[...] = jnp.logical_and(
@@ -220,6 +223,11 @@
         (tp_col >> 3) == 9 * (tp_row >> 4) + (tp_row & 15), (tp_row & 15) < 9
     ).astype(BF16)
 
+    load_vec.wait()
+    turned = vec[pl.ds(pl.multiple_of(HALF * h, HALF), HALF), :].T
+    for half in range(2):
+        vec_t[640 * half : 640 * half + HALF, :] = turned[HALF * half : HALF * half + HALF]
+        vec_t[640 * half + HALF : 640 * half + 640, :] = jnp.zeros((64, HALF), BF16)
     pltpu.make_async_copy(rx1, rx1, s1_recv).wait()
     arrived = jnp.concatenate([rx1[s] for s in range(16)], axis=0)
     wide = jnp.concatenate([arrived[32 * g : 32 * g + 32] for g in range(4)], axis=1).astype(BF16)
@@ -262,36 +270,29 @@
         return c
 
     lax.fori_loop(0, 15, hand_on, 0)
-    load_vec.wait()
 
     def wait_sibling(o, c):
         arrival(1 - core, source(o)).wait()
         return c
 
-    lax.fori_loop(0, 16, wait_sibling, 0)
-
     u_all = (iota((1280, 128), 0) & 7) == (iota((1280, 128), 1) >> 4)
-    parts = []
-    for half in range(2):
+
+    def spread_rows(half):
         main = jnp.concatenate([gathered[half, chip, 0:80] for chip in range(16)], axis=0)
         tail = jnp.concatenate([
             dot(tailsel[...], jnp.concatenate([gathered[half, 4 * g + k, 80:96] for k in range(4)], axis=0))
             for g in range(4)
         ], axis=0)
         tail = jnp.where(u_all, tail, 0.0).astype(BF16)
-        parts.append(jnp.concatenate([main, tail], axis=1))
-
-    def put(begin, end, value):
+        value = dot(jnp.concatenate([main, tail], axis=1), expand[half])
         value = jnp.concatenate([value[80 * k : 80 * k + CHIP] for k in range(16)], axis=0)
-        wide_goal = jnp.concatenate([colg[...]] * ((end - begin) // 128), axis=1)
-        keep = wide_goal == irr_ref[:, begin:end]
-        texp[:, begin:end] = jnp.where(keep, value, 0.0).astype(BF16)
-
-    put(0, 512, dot(parts[0], expand[0:256, 0:512]))
-    put(512, 768, dot(jnp.concatenate(parts, axis=1), expand[:, 512:768]))
-    put(768, 1152, dot(parts[1], expand[256:512, 768:1152]))
-    rows_h = vec[pl.ds(pl.multiple_of(HALF * h, HALF), HALF), :]
-    inner[...] = dot_nt(texp[...], rows_h).astype(BF16)
+        keep = jnp.concatenate([colg[...]] * 5, axis=1) == irrpad[pl.ds(half, 1), :]
+        texp[:, pl.ds(pl.multiple_of(640 * half, 128), 640)] = jnp.where(keep, value, 0.0).astype(BF16)
+
+    spread_rows(core)
+    lax.fori_loop(0, 16, wait_sibling, 0)
+    spread_rows(1 - core)
+    inner[...] = dot(texp[...], vec_t[...]).astype(BF16)
 
     def slot_of(d):
         return (d // 8) * 4 + d % 4
@@ -459,14 +460,16 @@
             pltpu.VMEM((CHIP, BLK), F32),
             pltpu.VMEM((CHIP, BLK), F32),
             pltpu.VMEM((128, BLK), BF16),
+            pltpu.VMEM((1280, HALF), BF16),
+            pltpu.VMEM((8, 640), I32),
             pltpu.VMEM((512, 768), BF16),
-            pltpu.VMEM((512, NV), BF16),
+            pltpu.VMEM((2, 256, 640), BF16),
             pltpu.VMEM((256, HALF), BF16),
             pltpu.VMEM((320, 64), BF16),
             pltpu.VMEM((4, 8, 128), F32),
             pltpu.VMEM((16, 8, 128), F32),
             pltpu.VMEM((2, 16, 96, 128), BF16),
-            pltpu.VMEM((NV, NV), BF16),
+            pltpu.VMEM((NV, 1280), BF16),
             pltpu.VMEM((NV, HALF), BF16),
             pltpu.VMEM((16, 96, 128), BF16),
             pltpu.VMEM((8, 96, 128), BF16),

time: 55.1 us -> 55.7 us (1.011)
  Pallas kernels: 53.5 us -> 54.1 us
    pallas_call x1, Pallas kernels: 53.5 us -> 54.1 us  [per_device(): pl.pallas_call(kernel, out_shape=jax.ShapeDtypeStruct(amplitudes.shape, B...]
where the time goes in v5:
time: 55.7 us; the launch traced here: 55.5 us
  Pallas kernels  54.1 us (97%)
  local copies, waits for them, and re-layouts  1.4 us (3%)
    pallas_call x1, Pallas kernels, per_device(): pl.pallas_call(kernel, out_shape=jax.ShapeDtypeStruct(amplitudes.shape, B...  54.1 us
    unnamed x1, local copies, waits for them, and re-layouts  1.4 us

profile of v5, /device:TPU:1, one launch (start us, length us, event | category | flops | bytes accessed | tf_op | source)
XLA Modules:
  0.0 55.5 jit_solution(16153889851573071864)
XLA Ops:
  0.0 54.1 %shard_map.46 = bf16[18,4,144]{2,1,0:T(4,128)(2,1)} custom-call(bf16[18,4,144]{2,1,0:T(4,128)(2,1)} %amp_hbm.1, bf16[1,1152,1152]{2,1,0:T(8,128)(2,1)} %chol_ref.1, s32[9,128]{1,0:T(8,128)} %bitcast.1, s32[4]{0:T(128)} %pair_hbm.1), custom_call_target="tpu_custom_call" | custom-call | flops 3060000000 | bytes 2700000 | tf_op jit(solution)/shard_map/pallas_call | solution.py:443
  54.1 1.4 %copy.6 = bf16[18,4,144]{2,1,0:T(4,128)(2,1)} copy(bf16[18,4,144]{2,1,0:T(4,128)(2,1)} %shard_map.46) | data formatting | bytes 41472
